TPU v7x, 32 devices: a whole 2x2x4 slice. The times are simulated.
32 devices in a mesh: lon: 4 (over y, x), sec: 8 (over z, core).
Axes of the slice: x: 2, y: 2, z: 4, core: 2. Of those that a mesh axis runs over, the one named last changes fastest.
Arguments:
- moisture: float32 [16, 128, 1024], P(None, 'sec', 'lon'), may hold values from 0 to 2
- heat: float32 [16, 128, 1024], P(None, 'sec', 'lon'), may hold values from -6 to 6
- moist_cond: float32 [16, 128, 1024], P(None, 'sec', 'lon'), may hold values from 0.05 to 2
- heat_cond: float32 [16, 128, 1024], P(None, 'sec', 'lon'), may hold values from 0.1 to 3
- rain: float32 [128, 1024], P('sec', 'lon'), may hold values from 0.01 to 1
- surface_flux: float32 [128, 1024], P('sec', 'lon'), may hold values from -6 to 6
- cell_reach: int32 [128, 1024], P('sec', 'lon'), may hold values from 0 to 16383
- records: bfloat16 [4, 16384, 256], P('lon', 'sec'), may hold values from 0 to 2
- unit_hydro: bfloat16 [4, 16384, 256], P('lon', 'sec'), may hold values from 0.049804688 to 1
- down_basin: int32 [4, 16384], P('lon', 'sec'), may hold values from 0 to 4095
- basin_home: int32 [4, 4096], P('lon'), may hold values from 0 to 4095, as said below
- send_index: int32 [4, 8, 8, 512], P('lon', 'sec'), may hold values from 0 to 2047, as said below
- send_count: int32 [4, 8, 8], P('lon', 'sec'), may hold values from 0 to 512, as said below
Outputs:
- moist_out: float32 [16, 128, 1024], P(None, 'sec', 'lon')
- heat_out: float32 [16, 128, 1024], P(None, 'sec', 'lon')
- record_out: bfloat16 [4, 16384, 256], P('lon', 'sec')
- basin_inflow: float32 [4, 4096, 256], P('lon', 'sec')
Inputs may be any that keep to these rules, and one draw needn't show every extreme that they name: `send_index`: within a longitude group, device s lists each of its 2048 reaches in exactly one used slot; a reach listed in block d drains into a basin whose basin_home lies in d * 512 to (d+1) * 512 - 1. Unused slots hold 0. `send_count`: in every group one owner receives 512 reaches from every device of sec; counts of owners 2 m and 2 m + 1 from one device add up to 512. `basin_home`: each group's row is a permutation.
All inputs are finite; a program needn't handle non-finite values.
Results may differ from a plain program's by a relative error of at most 0.009.
Values may be sent and summed in bfloat16 or wider, within the bound.
No kernel may reach another device: no remote copies, remote signals or barrier semaphores. Data moves between devices by JAX's collectives and lax.ppermute only.
A program may use at most 64 MiB of HBM per device.

v0:
```python
import jax
import jax.numpy as jnp
from jax import lax
from jax.sharding import PartitionSpec as P

LATERAL = 0.2


def extended(cells, sides, width):
    for axis, dim in sides:
        count = lax.axis_size(axis)
        ends = count - 1
        head = lax.slice_in_dim(cells, 0, width, axis=dim)
        tail = lax.slice_in_dim(cells, cells.shape[dim] - width, cells.shape[dim], axis=dim)
        cells = jnp.concatenate(
            [
                lax.ppermute(tail, axis, [(i, (i + 1) % count) for i in range(ends)]),
                cells,
                lax.ppermute(head, axis, [((i + 1) % count, i) for i in range(ends)]),
            ],
            axis=dim,
        )
    return cells


def column_solve(conduct, source):
    layer_count = conduct.shape[0]
    flat_zero = jnp.zeros_like(conduct[0])
    links = [0.5 * (conduct[layer] + conduct[layer + 1]) for layer in range(layer_count - 1)]
    above_link = links + [flat_zero]
    below_link = [flat_zero] + links
    prev_ratio = flat_zero
    prev_value = flat_zero
    ratio_list = []
    value_list = []
    for layer in range(layer_count):
        pivot_value = 1.0 + below_link[layer] + above_link[layer] + below_link[layer] * prev_ratio
        prev_ratio = -above_link[layer] / pivot_value
        prev_value = (source[layer] + below_link[layer] * prev_value) / pivot_value
        ratio_list.append(prev_ratio)
        value_list.append(prev_value)
    result = [None] * layer_count
    result[layer_count - 1] = value_list[layer_count - 1]
    for layer in range(layer_count - 2, -1, -1):
        result[layer] = value_list[layer] - ratio_list[layer] * result[layer + 1]
    return jnp.stack(result)


def per_device(
    moisture,
    heat,
    moist_cond,
    heat_cond,
    rain,
    surface_flux,
    cell_reach,
    records,
    unit_hydro,
    down_basin,
    basin_home,
    send_index,
    send_count,
):
    sections = lax.axis_size("sec")
    steps_count = records.shape[2]
    capacity = send_index.shape[3]
    basin_local = basin_home.shape[1] // sections
    rows_left = send_index[0, 0]
    usable = jnp.arange(capacity, dtype=jnp.int32)[None, :] < send_count[0, 0][:, None]
    home_slot = jnp.take(basin_home[0], down_basin[0])
    local_slot = home_slot % basin_local
    slot_ids = jnp.where(usable, jnp.take(local_slot, rows_left), -1)
    stacked = jnp.stack([moisture, heat])
    padded = extended(stacked.astype(jnp.bfloat16), (("lon", 3), ("sec", 2)), 1).astype(
        stacked.dtype
    )
    beside_all = (
        padded[:, :, 2:, 1:-1]
        + padded[:, :, :-2, 1:-1]
        + padded[:, :, 1:-1, 2:]
        + padded[:, :, 1:-1, :-2]
    )
    middle = stacked + LATERAL * (beside_all - 4.0 * stacked)
    moist_rhs = middle[0].at[0].add(rain)
    heat_rhs = middle[1].at[0].add(surface_flux)
    moist_out = column_solve(moist_cond, moist_rhs)
    heat_out = column_solve(heat_cond, heat_rhs)
    layer_last = moist_cond.shape[0] - 1
    runoff = (
        jax.nn.softplus(moist_out[0] - 1.0) * jax.nn.sigmoid(heat_out[0])
        + 0.5 * moist_cond[layer_last] * moist_out[layer_last]
    )
    reach_terms = jax.ops.segment_sum(
        runoff.reshape(-1), cell_reach.reshape(-1), num_segments=records.shape[1] * sections
    )
    reach_runoff = lax.psum_scatter(
        reach_terms.astype(jnp.bfloat16), "sec", scatter_dimension=0, tiled=True
    ).astype(jnp.float32)
    shifted = jnp.concatenate(
        [records[0][:, 1:].astype(jnp.float32), jnp.zeros((records.shape[1], 1), jnp.float32)],
        axis=1,
    )
    record_new = (shifted + reach_runoff[:, None] * unit_hydro[0].astype(jnp.float32)).astype(
        jnp.bfloat16
    )
    arrived, ids_got = (
        lax.all_to_all(record_new[rows_left], "sec", split_axis=0, concat_axis=0, tiled=True),
        lax.all_to_all(slot_ids, "sec", split_axis=0, concat_axis=0, tiled=True),
    )
    onehot = (ids_got.reshape(1, -1) == jnp.arange(basin_local, dtype=jnp.int32)[:, None]).astype(
        jnp.bfloat16
    )
    inflow = jnp.dot(onehot, arrived.reshape(-1, steps_count), preferred_element_type=jnp.float32)
    return (moist_out, heat_out, record_new[None], inflow[None])


def solution(mesh):
    placed = (
        P(None, "sec", "lon"),
        P(None, "sec", "lon"),
        P(None, "sec", "lon"),
        P(None, "sec", "lon"),
        P("sec", "lon"),
        P("sec", "lon"),
        P("sec", "lon"),
        P("lon", "sec", None),
        P("lon", "sec", None),
        P("lon", "sec"),
        P("lon", None),
        P("lon", "sec", None, None),
        P("lon", "sec", None),
    )
    return jax.shard_map(
        per_device,
        mesh=mesh,
        in_specs=placed,
        out_specs=(
            P(None, "sec", "lon"),
            P(None, "sec", "lon"),
            P("lon", "sec", None),
            P("lon", "sec", None),
        ),
        check_vma=False,
    )
```

profile of v0, /device:TPU:0, one launch (start us, length us, event | category | flops | bytes accessed | tf_op | source)
XLA Modules:
  0.0 193.5 jit_solution(1754617943910263347)
XLA Ops:
  0.6 1.1 fusion.8
  1.8 4.8 %collective-permute-start = (bf16[2,16,16,1]{3,2,1,0:T(8,128)(2,1)S(1)}, bf16[2,16,16,1]{3,2,1,0:T(8,128)(2,1)S(1)}, u32[]{:S(2)}, u32[]{:S(2)}) collective-permute-start(bf16[2,16,16,1]{3,2,1,0:T(8,128)(2,1)S(1)} %get-tuple-element.152), channel_id=1, source_target_pairs={{0,8},{8,16},{16,24},{1,9},{9,17},{17,25},{2,10},{10,18},{18,26},{... | collective-permute-start | bytes 3080 | tf_op jit(solution)/shard_map/ppermute | solution.py:17
  6.7 1.3 collective-permute-start.1
  8.0 0.7 compare_select_fusion.2
  8.7 0.7 fusion.13
  9.5 11.8 %gather_fusion = s32[2048]{0:T(1024)S(1)} fusion(s32[4096]{0:T(1024)S(1)} %bitcast.385, s32[2048]{0:T(1024)S(1)} %broadcast_clamp_fusion.1), kind=kCustom, calls=%fused_computation | custom fusion | bytes 24576 | tf_op jit(solution)/shard_map/jit(_take)/gather | solution.py:70
  21.4 23.0 %gather_fusion.1 = s32[4096]{0:T(1024)S(1)} fusion(s32[2048]{0:T(1024)S(1)} %add_select_fusion, s32[4096]{0:T(1024)S(1)} %broadcast_clamp_fusion), kind=kCustom, calls=%fused_computation.1 | custom fusion | bytes 49152 | tf_op jit(solution)/shard_map/jit(_take)/gather | solution.py:72
  44.4 0.7 compare_select_fusion.1
  45.1 4.9 %all-to-all-start = ((s32[8,1,512]{2,1,0:T(1,128)}), s32[8,1,512]{2,1,0:T(1,128)}, u32[]{:S(2)}, u32[]{:S(2)}) async-start(s32[8,1,512]{2,1,0:T(1,128)} %compare_select_fusion.1), calls=%async_computation | async-start | bytes 32768 | tf_op jit(solution)/shard_map/all_to_all | solution.py:108
  50.0 0.9 pad_maximum_fusion.3
  50.9 2.5 %collective-permute-start.2 = (bf16[2,16,1,258]{3,2,1,0:T(2,128)(2,1)}, bf16[2,16,1,258]{3,2,1,0:T(2,128)(2,1)S(1)}, u32[]{:S(2)}, u32[]{:S(2)}) collective-permute-start(bf16[2,16,1,258]{3,2,1,0:T(2,128)(2,1)} %get-tuple-element.150), channel_id=1, source_target_pairs={{0,1},{1,2},{2,3},{3,4},{4,5},{5,6},{6,7},{8,9},{9,10},{10,11},{11... | collective-permute-start | bytes 49544 | tf_op jit(solution)/shard_map/ppermute | solution.py:17
  53.5 1.3 collective-permute-start.3
  57.1 0.8 collective-permute-done.3
  60.6 0.8 constant_dynamic-update-slice_fusion.31
  63.6 0.8 constant_dynamic-update-slice_fusion.15
  64.7 21.9 %scatter_custom_fusion = f32[16384]{0:T(1024)S(1)} fusion(s32[4096]{0:T(1024)S(1)} %bitcast.490, f32[4096]{0:T(1024)S(1)} %fusion.12, f32[]{:T(128)} %constant.102.clone.1), kind=kCustom, calls=%fused_computation.61 | custom fusion | flops 4096 | bytes 65540 | tf_op jit(solution)/shard_map/scatter-add | solution.py:93
  86.7 29.2 %all-reduce.1 = bf16[16384]{0:T(1024)(128)(2,1)S(1)} all-reduce(bf16[16384]{0:T(1024)(128)(2,1)S(1)} %convert_element_type.25), channel_id=2, replica_groups=mesh['lon'=4,'sec'=8] {'sec'}, use_global_device_ids=true, to_apply=%region_1.2.clone | all-reduce | flops 16384 | bytes 65536
  116.6 1.7 fusion.3
  118.3 0.7 constant_dynamic-update-slice_fusion.26
  119.0 16.9 %gather_fusion.2 = bf16[4096,256]{1,0:T(8,128)(2,1)} fusion(bf16[2048,256]{1,0:T(8,128)(2,1)S(1)} %fusion.3, s32[4096]{0:T(1024)S(1)} %copy-done.55), kind=kCustom, calls=%fused_computation.2 | custom fusion | bytes 4210688 | tf_op jit(solution)/shard_map/gather | solution.py:107
  136.2 4.5 %all-to-all-start.1 = ((bf16[8,512,256]{2,1,0:T(8,128)(2,1)}), bf16[8,512,256]{2,1,0:T(8,128)(2,1)}, u32[]{:S(2)}, u32[]{:S(2)}) async-start(bf16[8,512,256]{2,1,0:T(8,128)(2,1)} %bitcast.47), calls=%async_computation.1 | async-start | bytes 4194304 | tf_op jit(solution)/shard_map/all_to_all | solution.py:107
  145.9 0.6 constant_dynamic-update-slice_fusion.17
  147.2 42.6 %all-to-all-done.1 = bf16[8,512,256]{2,1,0:T(8,128)(2,1)} async-done(((bf16[8,512,256]{2,1,0:T(8,128)(2,1)}), bf16[8,512,256]{2,1,0:T(8,128)(2,1)}, u32[]{:S(2)}, u32[]{:S(2)}) %all-to-all-start.1) | async-done | bytes 2097184 | tf_op jit(solution)/shard_map/all_to_all | solution.py:107
  189.8 3.8 %fusion.4 = f32[1,512,256]{2,1,0:T(8,128)} fusion(bf16[4096,256]{1,0:T(8,128)(2,1)} %bitcast.48, s32[4096]{0:T(1024)} %bitcast.46), kind=kOutput, calls=%fused_computation.10 | convolution fusion | flops 1075838976 | bytes 2637824 | tf_op jit(solution)/shard_map/dot_general | solution.py:113
  (241 shorter events, 12.6 us)
Async XLA Ops:
  1.8 48.2 %collective-permute-start = (bf16[2,16,16,1]{3,2,1,0:T(8,128)(2,1)S(1)}, bf16[2,16,16,1]{3,2,1,0:T(8,128)(2,1)S(1)}, u32[]{:S(2)}, u32[]{:S(2)}) collective-permute-start(bf16[2,16,16,1]{3,2,1,0:T(8,128)(2,1)S(1)} %get-tuple-element.152), channel_id=1, source_target_pairs={{0,8},{8,16},{16,24},{1,9},{9,17},{17,25},{2,10},{10,18},{18,26},{... | collective-permute-start | bytes 3080 | tf_op jit(solution)/shard_map/ppermute | solution.py:17
  6.7 43.3 %collective-permute-start.1 = (bf16[2,16,16,1]{3,2,1,0:T(8,128)(2,1)S(1)}, bf16[2,16,16,1]{3,2,1,0:T(8,128)(2,1)S(1)}, u32[]{:S(2)}, u32[]{:S(2)}) collective-permute-start(bf16[2,16,16,1]{3,2,1,0:T(8,128)(2,1)S(1)} %get-tuple-element.153), channel_id=1, source_target_pairs={{8,0},{16,8},{24,16},{9,1},{17,9},{25,17},{10,2},{18,10},{26,18},{... | collective-permute-start | bytes 3080 | tf_op jit(solution)/shard_map/ppermute | solution.py:19
  9.5 11.8 %copy-start.54 = (s32[4096]{0:T(1024)}, s32[4096]{0:T(1024)S(1)}, u32[]{:S(2)}) copy-start(s32[4096]{0:T(1024)S(1)} %broadcast_clamp_fusion) | copy-start | bytes 49156
  9.5 11.8 %copy-start.59 = (s32[1,2048]{1,0:T(1,128)S(1)}, s32[1,2048]{1,0:T(1,128)}, u32[]{:S(2)}) copy-start(s32[1,2048]{1,0:T(1,128)} %param.26) | copy-start | bytes 24580
  21.3 23.1 %copy-start.57 = (s32[1,1,8,512]{3,2,1,0:T(8,128)S(1)}, s32[1,1,8,512]{3,2,1,0:T(8,128)}, u32[]{:S(2)}) copy-start(s32[1,1,8,512]{3,2,1,0:T(8,128)} %param.28) | copy-start | bytes 49156
  21.3 23.1 %copy-start.63 = (s32[1,1,8]{2,1,0:T(1,128)S(1)}, s32[1,1,8]{2,1,0:T(1,128)}, u32[]{:S(2)}) copy-start(s32[1,1,8]{2,1,0:T(1,128)} %param.29) | copy-start | bytes 100
  21.3 33.4 %copy-start.5 = (f32[16,16,256]{2,1,0:T(8,128)S(1)}, f32[16,16,256]{2,1,0:T(8,128)}, u32[]{:S(2)}) copy-start(f32[16,16,256]{2,1,0:T(8,128)} %param.19) | copy-start | bytes 786436
  21.3 33.4 %copy-start.60 = (s32[16,256]{1,0:T(8,128)S(1)}, s32[16,256]{1,0:T(8,128)}, u32[]{:S(2)}) copy-start(s32[16,256]{1,0:T(8,128)} %param.23) | copy-start | bytes 49156
  21.4 34.1 %copy-start.4 = (bf16[1,2048,256]{2,1,0:T(8,128)(2,1)S(1)}, bf16[1,2048,256]{2,1,0:T(8,128)(2,1)}, u32[]{:S(2)}) copy-start(bf16[1,2048,256]{2,1,0:T(8,128)(2,1)} %param.24) | copy-start | bytes 3145732
  45.1 90.8 %all-to-all-start = ((s32[8,1,512]{2,1,0:T(1,128)}), s32[8,1,512]{2,1,0:T(1,128)}, u32[]{:S(2)}, u32[]{:S(2)}) async-start(s32[8,1,512]{2,1,0:T(1,128)} %compare_select_fusion.1), calls=%async_computation | async-start | bytes 32768 | tf_op jit(solution)/shard_map/all_to_all | solution.py:108
  50.9 6.2 %collective-permute-start.2 = (bf16[2,16,1,258]{3,2,1,0:T(2,128)(2,1)}, bf16[2,16,1,258]{3,2,1,0:T(2,128)(2,1)S(1)}, u32[]{:S(2)}, u32[]{:S(2)}) collective-permute-start(bf16[2,16,1,258]{3,2,1,0:T(2,128)(2,1)} %get-tuple-element.150), channel_id=1, source_target_pairs={{0,1},{1,2},{2,3},{3,4},{4,5},{5,6},{6,7},{8,9},{9,10},{10,11},{11... | collective-permute-start | bytes 49544 | tf_op jit(solution)/shard_map/ppermute | solution.py:17
  53.5 4.5 %collective-permute-start.3 = (bf16[2,16,1,258]{3,2,1,0:T(2,128)(2,1)}, bf16[2,16,1,258]{3,2,1,0:T(2,128)(2,1)S(1)}, u32[]{:S(2)}, u32[]{:S(2)}) collective-permute-start(bf16[2,16,1,258]{3,2,1,0:T(2,128)(2,1)} %get-tuple-element.151), channel_id=1, source_target_pairs={{1,0},{2,1},{3,2},{4,3},{5,4},{6,5},{7,6},{9,8},{10,9},{11,10},{12... | collective-permute-start | bytes 49544 | tf_op jit(solution)/shard_map/ppermute | solution.py:19
  60.3 26.4 %copy-start.31 = (f32[1,16,256]{2,1,0:T(8,128)}, f32[1,16,256]{2,1,0:T(8,128)S(1)}, u32[]{:S(2)}) copy-start(f32[1,16,256]{2,1,0:T(8,128)S(1)} %get-tuple-element.41) | copy-start | bytes 49156
  60.3 26.4 %copy-start.33 = (f32[1,16,256]{2,1,0:T(8,128)}, f32[1,16,256]{2,1,0:T(8,128)S(1)}, u32[]{:S(2)}) copy-start(f32[1,16,256]{2,1,0:T(8,128)S(1)} %get-tuple-element.45) | copy-start | bytes 49156
  60.3 26.4 %copy-start.35 = (f32[1,16,256]{2,1,0:T(8,128)}, f32[1,16,256]{2,1,0:T(8,128)S(1)}, u32[]{:S(2)}) copy-start(f32[1,16,256]{2,1,0:T(8,128)S(1)} %get-tuple-element.46) | copy-start | bytes 49156
  60.3 26.4 %copy-start.37 = (f32[1,16,256]{2,1,0:T(8,128)}, f32[1,16,256]{2,1,0:T(8,128)S(1)}, u32[]{:S(2)}) copy-start(f32[1,16,256]{2,1,0:T(8,128)S(1)} %get-tuple-element.50) | copy-start | bytes 49156
  60.3 26.4 %copy-start.39 = (f32[1,16,256]{2,1,0:T(8,128)}, f32[1,16,256]{2,1,0:T(8,128)S(1)}, u32[]{:S(2)}) copy-start(f32[1,16,256]{2,1,0:T(8,128)S(1)} %get-tuple-element.51) | copy-start | bytes 49156
  60.3 26.4 %copy-start.41 = (f32[1,16,256]{2,1,0:T(8,128)}, f32[1,16,256]{2,1,0:T(8,128)S(1)}, u32[]{:S(2)}) copy-start(f32[1,16,256]{2,1,0:T(8,128)S(1)} %get-tuple-element.55) | copy-start | bytes 49156
  60.3 26.4 %copy-start.43 = (f32[1,16,256]{2,1,0:T(8,128)}, f32[1,16,256]{2,1,0:T(8,128)S(1)}, u32[]{:S(2)}) copy-start(f32[1,16,256]{2,1,0:T(8,128)S(1)} %get-tuple-element.56) | copy-start | bytes 49156
  61.4 55.2 %copy-start.49 = (f32[1,16,256]{2,1,0:T(8,128)}, f32[1,16,256]{2,1,0:T(8,128)S(1)}, u32[]{:S(2)}) copy-start(f32[1,16,256]{2,1,0:T(8,128)S(1)} %get-tuple-element.31) | copy-start | bytes 49156
  64.4 54.6 %copy-start.55 = (s32[4096]{0:T(1024)S(1)}, s32[4096]{0:T(1024)}, u32[]{:S(2)}) copy-start(s32[4096]{0:T(1024)} %copy-done.54) | copy-start | bytes 49156
  118.3 17.6 %copy-start.1 = (bf16[2048,256]{1,0:T(8,128)(2,1)}, bf16[2048,256]{1,0:T(8,128)(2,1)S(1)}, u32[]{:S(2)}) copy-start(bf16[2048,256]{1,0:T(8,128)(2,1)S(1)} %fusion.3) | copy-start | bytes 3145732
  136.2 53.6 %all-to-all-start.1 = ((bf16[8,512,256]{2,1,0:T(8,128)(2,1)}), bf16[8,512,256]{2,1,0:T(8,128)(2,1)}, u32[]{:S(2)}, u32[]{:S(2)}) async-start(bf16[8,512,256]{2,1,0:T(8,128)(2,1)} %bitcast.47), calls=%async_computation.1 | async-start | bytes 4194304 | tf_op jit(solution)/shard_map/all_to_all | solution.py:107
  147.2 46.3 %copy-start.62 = (f32[16,16,256]{2,1,0:T(8,128)}, f32[16,16,256]{2,1,0:T(8,128)S(1)}, u32[]{:S(2)}) copy-start(f32[16,16,256]{2,1,0:T(8,128)S(1)} %get-tuple-element.147) | copy-start | bytes 786436
  (47 other events, 297.6 us)
where the time goes:
time: 195 us; the launch traced here: 194 us
  local copies, waits for them, and re-layouts  58.9 us (30%)
  waiting for transfers between devices  43.4 us (22%)
  other arithmetic  36 us (18%)
  blocking collectives  29.2 us (15%)
  starting transfers between devices  19.3 us (10%)
  matrix products  3.77 us (2%)
  between operations  2.91 us (1%)
    all_to_all x1, waiting for transfers between devices, per_device(): lax.all_to_all(record_new[rows_left], 'sec', split_axis=0, concat_axis=0,...  42.6 us
    unnamed x1, blocking collectives  29.2 us
    gather x1, local copies, waits for them, and re-layouts, per_device(): slot_ids = jnp.where(usable, jnp.take(local_slot, rows_left), -1)  23 us
    scatter-add x1, other arithmetic, per_device(): jax.ops.segment_sum(runoff.reshape(-1), cell_reach.reshape(-1), num_segme...  21.9 us
    gather x1, local copies, waits for them, and re-layouts, per_device(): record_new[rows_left]  16.9 us
    gather x1, local copies, waits for them, and re-layouts, per_device(): home_slot = jnp.take(basin_home[0], down_basin[0])  11.8 us
    ppermute x2, starting transfers between devices, extended(): lax.ppermute(tail, axis, [(i, (i + 1) % count) for i in range(ends)])  7.37 us
    unnamed x18, other arithmetic  6.63 us
  transfers between devices with their start and end apart: 6, of which 2 were waited for; matrix products, arithmetic and copies ran while one was open for 48% of the time, Pallas kernels for 0%

commit v1 on v0

v1 whole, which is shorter than its diff:
```python
import functools

import jax
import jax.numpy as jnp
from jax import lax
from jax.experimental import pallas as pl
from jax.experimental.pallas import tpu as pltpu
from jax.sharding import PartitionSpec as P

LATERAL = 0.2
LANES = 128
F32 = jnp.float32
BF16 = jnp.bfloat16


def params(mib=48):
    return pltpu.CompilerParams(vmem_limit_bytes=mib * 1024 * 1024)


def call(body, outs, *args, smem=(), flops=0, moved=0):
    specs = [
        pl.BlockSpec(memory_space=pltpu.SMEM if i in smem else pltpu.VMEM)
        for i in range(len(args))
    ]
    single = not isinstance(outs, (list, tuple))
    out_list = [outs] if single else list(outs)
    result = pl.pallas_call(
        body,
        out_shape=out_list,
        in_specs=specs,
        out_specs=[pl.BlockSpec(memory_space=pltpu.VMEM) for _ in out_list],
        compiler_params=params(),
        cost_estimate=pl.CostEstimate(flops=flops, bytes_accessed=moved, transcendentals=0),
    )(*args)
    return result[0] if single else result


def edges_body(moist, heat, north, south, west, east):
    layers, rows, cols = moist.shape
    lane = lax.broadcasted_iota(jnp.int32, (rows, LANES), 1)
    west_all = jnp.zeros((rows, LANES), F32)
    east_all = jnp.zeros((rows, LANES), F32)
    for f, ref in enumerate((moist, heat)):
        north[f * layers : (f + 1) * layers, :] = ref[:, 0, :].astype(BF16)
        south[f * layers : (f + 1) * layers, :] = ref[:, rows - 1, :].astype(BF16)
        for layer in range(layers):
            k = f * layers + layer
            west_all = jnp.where(lane == k, ref[layer, :, 0:1], west_all)
            east_all = jnp.where(lane == k, ref[layer, :, cols - 1 : cols], east_all)
    west[...] = west_all.astype(BF16)
    east[...] = east_all.astype(BF16)


def lookup(table, hi, lo):
    out = jnp.zeros(hi.shape, table.dtype)
    for row in range(table.shape[0]):
        line = jnp.broadcast_to(table[row : row + 1, :], hi.shape)
        got = jnp.take_along_axis(line, lo, axis=1)
        out = jnp.where(hi == row, got, out)
    return out


def index_body(listed, count, home, down, order, place):
    pairs, width = order.shape
    pos = lax.broadcasted_iota(jnp.int32, (1, width), 1)
    for m in range(pairs):
        c = count[2 * m]
        first = listed[m : m + 1, :width]
        second = pltpu.roll(listed[m : m + 1, width:], lax.rem(c, width), 1)
        order[m : m + 1, :] = jnp.where(pos < c, first, second)
    slot = lookup(home[...], down[...] >> 7, down[...] & (LANES - 1))
    for t in range(width // LANES):
        at = order[:, t * LANES : (t + 1) * LANES]
        place[:, t * LANES : (t + 1) * LANES] = lookup(slot, at >> 7, at & (LANES - 1))


def shift_time(x):
    steps = x.shape[1]
    lane = lax.broadcasted_iota(jnp.int32, x.shape, 1)
    return jnp.where(lane == steps - 1, 0.0, pltpu.roll(x, steps - 1, 1))


def pack_body(order, records, hydro, rec_packed, hyd_packed):
    tiles = order.shape[0]
    reaches = records.shape[0]
    turned = order[...].astype(F32).T
    group = 4
    for g in range(tiles // group):
        lane = lax.broadcasted_iota(jnp.int32, (LANES, reaches), 1).astype(F32)
        hot = jnp.concatenate(
            [
                jnp.where(lane == turned[:, g * group + i : g * group + i + 1], 1.0, 0.0).astype(BF16)
                for i in range(group)
            ],
            axis=0,
        )
        at = pl.ds(g * group * LANES, group * LANES)
        rec = jnp.dot(hot, records[...], preferred_element_type=F32)
        rec_packed[at, :] = shift_time(rec).astype(BF16)
        hyd_packed[at, :] = jnp.dot(hot, hydro[...], preferred_element_type=F32).astype(BF16)


def land_body(
    moist, heat, moist_k, heat_k, rain, flux, cell, north, south, west, east, ids,
    moist_out, heat_out, terms,
):
    layers, rows, cols = moist.shape
    row = lax.broadcasted_iota(jnp.int32, (rows, cols), 0)
    col = lax.broadcasted_iota(jnp.int32, (rows, cols), 1)
    north_all = north[...].astype(F32)
    south_all = south[...].astype(F32)
    west_all = west[...].astype(F32)
    east_all = east[...].astype(F32)
    for f, (x_ref, k_ref, top, out) in enumerate(
        ((moist, moist_k, rain, moist_out), (heat, heat_k, flux, heat_out))
    ):
        ratio = jnp.zeros((rows, cols), F32)
        value = jnp.zeros((rows, cols), F32)
        below = jnp.zeros((rows, cols), F32)
        ratios, values = [], []
        for layer in range(layers):
            k = f * layers + layer
            x = x_ref[layer]
            up = jnp.where(row == 0, north_all[k : k + 1, :], pltpu.roll(x, 1, 0))
            dn = jnp.where(row == rows - 1, south_all[k : k + 1, :], pltpu.roll(x, rows - 1, 0))
            lf = jnp.where(col == 0, west_all[:, k : k + 1], pltpu.roll(x, 1, 1))
            rt = jnp.where(col == cols - 1, east_all[:, k : k + 1], pltpu.roll(x, cols - 1, 1))
            rhs = x + LATERAL * (up + dn + lf + rt - 4.0 * x)
            if layer == 0:
                rhs = rhs + top[...]
            if layer < layers - 1:
                above = 0.5 * (k_ref[layer] + k_ref[layer + 1])
            else:
                above = jnp.zeros((rows, cols), F32)
            inv = 1.0 / (1.0 + below + above + below * ratio)
            ratio = -above * inv
            value = (rhs + below * value) * inv
            ratios.append(ratio)
            values.append(value)
            below = above
        x = values[-1]
        out[layers - 1] = x
        for layer in range(layers - 2, -1, -1):
            x = values[layer] - ratios[layer] * x
            out[layer] = x
    s = moist_out[0] - 1.0
    soft = jnp.maximum(s, 0.0) + jnp.log1p(jnp.exp(-jnp.abs(s)))
    gate = 1.0 / (1.0 + jnp.exp(-heat_out[0]))
    runoff = soft * gate + 0.5 * moist_k[layers - 1] * moist_out[layers - 1]
    cells = cell[...]
    hi = cells >> 7
    lo = cells & (LANES - 1)
    sections, blocks = terms.shape[0], terms.shape[1] - ids.shape[1]
    his = sections * blocks
    hi_iota = lax.broadcasted_iota(jnp.int32, (his, cols), 0)
    lo_iota = lax.broadcasted_iota(jnp.int32, (LANES, cols), 0)
    acc = jnp.zeros((his, LANES), F32)
    for i in range(rows):
        a = jnp.where(hi_iota == hi[i : i + 1, :], runoff[i : i + 1, :], 0.0).astype(BF16)
        b = jnp.where(lo_iota == lo[i : i + 1, :], 1.0, 0.0).astype(BF16)
        acc = acc + lax.dot_general(a, b, (((1,), (1,)), ((), ())), preferred_element_type=F32)
    terms[:, :blocks, :] = acc.reshape(sections, blocks, LANES).astype(BF16)
    terms[:, blocks:, :] = ids[...]


def send_body(got, order, rec_packed, hyd_packed, ready, runoff):
    blocks = runoff.shape[0]
    total = jnp.sum(got[:, :blocks, :].astype(F32), axis=0)
    runoff[...] = total
    at = order[...]
    turned = lookup(total, at >> 7, at & (LANES - 1)).T
    for t in range(blocks):
        rows = pl.ds(t * LANES, LANES)
        ready[rows, :] = (
            rec_packed[rows, :].astype(F32) + turned[:, t : t + 1] * hyd_packed[rows, :].astype(F32)
        ).astype(BF16)


def record_body(runoff, records, hydro, out):
    turned = runoff[...].T
    for t in range(runoff.shape[0]):
        rows = pl.ds(t * LANES, LANES)
        out[rows, :] = (
            shift_time(records[rows, :].astype(F32)) + turned[:, t : t + 1] * hydro[rows, :].astype(F32)
        ).astype(BF16)


def basin_body(place, rows, out):
    basins = out.shape[0]
    slot = lax.broadcasted_iota(jnp.int32, (basins, LANES), 0).astype(F32)
    hot = jnp.concatenate(
        [
            jnp.where(slot == place[t : t + 1, :], 1.0, 0.0).astype(BF16)
            for t in range(place.shape[0])
        ],
        axis=1,
    )
    out[...] = jnp.dot(hot, rows[...], preferred_element_type=F32).astype(out.dtype)


def per_device(
    moisture, heat, moist_cond, heat_cond, rain, surface_flux, cell_reach,
    records, unit_hydro, down_basin, basin_home, send_index, send_count,
):
    lons = lax.axis_size("lon")
    sections = lax.axis_size("sec")
    layers, lats, cols = moisture.shape
    reaches, steps = records.shape[1:]
    cap = send_index.shape[3]
    half = cap // 2
    pairs = sections // 2
    basins = basin_home.shape[1] // sections
    blocks = reaches // LANES
    shape = jax.ShapeDtypeStruct

    north, south, west, east = call(
        edges_body,
        [
            shape((2 * layers, cols), BF16),
            shape((2 * layers, cols), BF16),
            shape((lats, LANES), BF16),
            shape((lats, LANES), BF16),
        ],
        moisture,
        heat,
        moved=moisture.size * 8,
    )
    up_lon = [(i, i + 1) for i in range(lons - 1)]
    dn_lon = [(i + 1, i) for i in range(lons - 1)]
    up_sec = [(i, i + 1) for i in range(sections - 1)]
    dn_sec = [(i + 1, i) for i in range(sections - 1)]
    from_north = lax.ppermute(south, "sec", up_sec)
    from_south = lax.ppermute(north, "sec", dn_sec)
    from_west = lax.ppermute(east, "lon", up_lon)
    from_east = lax.ppermute(west, "lon", dn_lon)

    order, home_slot = call(
        index_body,
        [shape((pairs, cap), jnp.int32), shape((pairs, cap), jnp.int32)],
        send_index.reshape(pairs, 2 * cap),
        send_count.reshape(sections),
        basin_home.reshape(-1, LANES),
        down_basin.reshape(-1, LANES),
        smem=(1,),
        moved=sections * cap * 16,
    )
    order = order.reshape(-1, LANES)
    chip_place = home_slot - (2 * basins) * jnp.arange(pairs, dtype=jnp.int32)[:, None]
    digits = jnp.stack(
        [(chip_place >> 8).reshape(sections, half), (chip_place & 255).reshape(sections, half)], axis=1
    ).astype(BF16)
    id_rows = -(-(2 * half) // (16 * LANES)) * 16
    ids = jnp.pad(
        digits.reshape(sections, 2 * half), ((0, 0), (0, id_rows * LANES - 2 * half))
    ).reshape(sections, id_rows, LANES)

    rec_packed, hyd_packed = call(
        pack_body,
        [shape((reaches, steps), BF16), shape((reaches, steps), BF16)],
        order,
        records[0],
        unit_hydro[0],
        flops=4 * reaches * reaches * steps,
        moved=reaches * steps * 8,
    )

    moist_out, heat_out, terms = call(
        land_body,
        [
            shape(moisture.shape, F32),
            shape(heat.shape, F32),
            shape((sections, blocks + id_rows, LANES), BF16),
        ],
        moisture, heat, moist_cond, heat_cond, rain, surface_flux, cell_reach,
        from_north, from_south, from_west, from_east, ids,
        moved=moisture.size * 24,
    )

    got = lax.all_to_all(terms, "sec", split_axis=0, concat_axis=0, tiled=True)
    ready, runoff = call(
        send_body,
        [shape((reaches, steps), BF16), shape((blocks, LANES), F32)],
        got,
        order,
        rec_packed,
        hyd_packed,
        moved=reaches * steps * 6,
    )
    arrived = lax.all_to_all(
        ready.reshape(sections, half, steps), "sec", split_axis=0, concat_axis=0, tiled=True
    ).reshape(reaches, steps)

    record_new = call(
        record_body,
        shape((reaches, steps), BF16),
        runoff,
        records[0],
        unit_hydro[0],
        moved=reaches * steps * 6,
    )
    id_digits = (
        got[:, blocks:, :].astype(F32).reshape(sections, id_rows * LANES)[:, : 2 * half].reshape(sections, 2, half)
    )
    spot = (id_digits[:, 0] * 256.0 + id_digits[:, 1]).reshape(-1, LANES)
    core = (lax.axis_index("sec") % 2).astype(F32)
    theirs = call(
        basin_body,
        shape((basins, steps), BF16),
        spot - (1.0 - core) * basins,
        arrived,
        flops=2 * basins * reaches * steps,
        moved=reaches * steps * 2,
    )
    passed = lax.ppermute(theirs, "sec", [(i, i ^ 1) for i in range(sections)])
    mine = call(
        basin_body,
        shape((basins, steps), F32),
        spot - core * basins,
        arrived,
        flops=2 * basins * reaches * steps,
        moved=reaches * steps * 2,
    )
    inflow = mine + passed.astype(F32)
    return (moist_out, heat_out, record_new[None], inflow[None])


def solution(mesh):
    placed = (
        P(None, "sec", "lon"),
        P(None, "sec", "lon"),
        P(None, "sec", "lon"),
        P(None, "sec", "lon"),
        P("sec", "lon"),
        P("sec", "lon"),
        P("sec", "lon"),
        P("lon", "sec", None),
        P("lon", "sec", None),
        P("lon", "sec"),
        P("lon", None),
        P("lon", "sec", None, None),
        P("lon", "sec", None),
    )
    return jax.shard_map(
        per_device,
        mesh=mesh,
        in_specs=placed,
        out_specs=(
            P(None, "sec", "lon"),
            P(None, "sec", "lon"),
            P("lon", "sec", None),
            P("lon", "sec", None),
        ),
        check_vma=False,
    )
```

time: 195 us -> 78.5 us (0.40)
  the two profiles are of different devices: /device:TPU:0 before, /device:TPU:5 now
where the time goes in v1:
time: 78.5 us; the launch traced here: 77.7 us
  waiting for transfers between devices  25.7 us (33%)
  starting transfers between devices  24 us (31%)
  local copies, waits for them, and re-layouts  14 us (18%)
  Pallas kernels  11.2 us (14%)
  other arithmetic  1.9 us (2%)
  between operations  0.87 us (1%)
    all_to_all x1, waiting for transfers between devices, per_device(): lax.all_to_all(ready.reshape(sections, half, steps), 'sec', split_axis=0,...  25.7 us
    unnamed x38, local copies, waits for them, and re-layouts  13.2 us
    pallas_call x8, Pallas kernels, call(): pl.pallas_call(body, out_shape=out_list, in_specs=specs, out_specs=[pl.Bl...  11.2 us
    all_to_all x1, starting transfers between devices, per_device(): got = lax.all_to_all(terms, 'sec', split_axis=0, concat_axis=0, tiled=True)  5.99 us
    all_to_all x1, starting transfers between devices, per_device(): lax.all_to_all(ready.reshape(sections, half, steps), 'sec', split_axis=0,...  5.1 us
    ppermute x1, starting transfers between devices, per_device(): from_north = lax.ppermute(south, 'sec', up_sec)  3.9 us
    ppermute x1, starting transfers between devices, per_device(): from_west = lax.ppermute(east, 'lon', up_lon)  3.12 us
    ppermute x1, starting transfers between devices, per_device(): from_east = lax.ppermute(west, 'lon', dn_lon)  3.06 us
  transfers between devices with their start and end apart: 7, of which 1 were waited for; matrix products, arithmetic and copies ran while one was open for 1% of the time, Pallas kernels for 10%

profile of v1, /device:TPU:5, one launch (start us, length us, event | category | flops | bytes accessed | tf_op | source)
XLA Modules:
  0.0 77.7 jit_solution(11063772626476899536)
XLA Ops:
  0.7 1.0 %copy-done.5 = f32[16,16,256]{2,1,0:T(8,128)S(1)} copy-done((f32[16,16,256]{2,1,0:T(8,128)S(1)}, f32[16,16,256]{2,1,0:T(8,128)}, u32[]{:S(2)}) %copy-start.5) | copy-done | bytes 262168
  1.7 0.9 %copy-done.7 = f32[16,16,256]{2,1,0:T(8,128)S(1)} copy-done((f32[16,16,256]{2,1,0:T(8,128)S(1)}, f32[16,16,256]{2,1,0:T(8,128)}, u32[]{:S(2)}) %copy-start.7) | copy-done | bytes 262168
  2.8 3.9 %collective-permute-start = (bf16[32,256]{1,0:T(8,128)(2,1)S(1)}, bf16[32,256]{1,0:T(8,128)(2,1)S(1)}, u32[]{:S(2)}, u32[]{:S(2)}) collective-permute-start(bf16[32,256]{1,0:T(8,128)(2,1)S(1)} %get-tuple-element.17), channel_id=1, source_target_pairs={{0,1},{1,2},{2,3},{3,4},{4,5},{5,6},{6,7},{8,9},{9,10},{10,11},{11... | collective-permute-start | bytes 49160 | tf_op jit(solution)/shard_map/ppermute | solution.py:232
  6.7 1.9 %collective-permute-start.1 = (bf16[32,256]{1,0:T(8,128)(2,1)S(1)}, bf16[32,256]{1,0:T(8,128)(2,1)S(1)}, u32[]{:S(2)}, u32[]{:S(2)}) collective-permute-start(bf16[32,256]{1,0:T(8,128)(2,1)S(1)} %get-tuple-element.18), channel_id=1, source_target_pairs={{1,0},{2,1},{3,2},{4,3},{5,4},{6,5},{7,6},{9,8},{10,9},{11,10},{12... | collective-permute-start | bytes 49160 | tf_op jit(solution)/shard_map/ppermute | solution.py:233
  8.6 3.1 %collective-permute-start.2 = (bf16[16,128]{1,0:T(8,128)(2,1)S(1)}, bf16[16,128]{1,0:T(8,128)(2,1)S(1)}, u32[]{:S(2)}, u32[]{:S(2)}) collective-permute-start(bf16[16,128]{1,0:T(8,128)(2,1)S(1)} %get-tuple-element.19), channel_id=1, source_target_pairs={{0,8},{8,16},{16,24},{1,9},{9,17},{17,25},{2,10},{10,18},{18,26},{... | collective-permute-start | bytes 12296 | tf_op jit(solution)/shard_map/ppermute | solution.py:234
  11.8 3.1 %collective-permute-start.3 = (bf16[16,128]{1,0:T(8,128)(2,1)S(1)}, bf16[16,128]{1,0:T(8,128)(2,1)S(1)}, u32[]{:S(2)}, u32[]{:S(2)}) collective-permute-start(bf16[16,128]{1,0:T(8,128)(2,1)S(1)} %get-tuple-element.20), channel_id=1, source_target_pairs={{8,0},{16,8},{24,16},{9,1},{17,9},{25,17},{10,2},{18,10},{26,18},{... | collective-permute-start | bytes 12296 | tf_op jit(solution)/shard_map/ppermute | solution.py:235
  14.8 0.7 reshape.60.listed
  17.7 0.9 %shard_map.157 = (s32[4,512]{1,0:T(4,128)S(1)}, s32[4,512]{1,0:T(4,128)S(1)}) custom-call(s32[4,1024]{1,0:T(4,128)S(1)} %reshape.60.listed, s32[8]{0:T(128)S(1)} %bitcast.39, s32[32,128]{1,0:T(8,128)S(1)} %bitcast.37, s32[16,128]{1,0:T(8,128)S(1)} %bitcast.38), custom_call_target="tpu_custom_call" | custom-call | bytes 65536 | tf_op jit(solution)/shard_map/pallas_call | solution.py:27
  18.8 0.9 %copy-done.6 = f32[16,16,256]{2,1,0:T(8,128)S(1)} copy-done((f32[16,16,256]{2,1,0:T(8,128)S(1)}, f32[16,16,256]{2,1,0:T(8,128)}, u32[]{:S(2)}) %copy-start.6) | copy-done | bytes 262168
  19.7 0.9 %copy-done.8 = f32[16,16,256]{2,1,0:T(8,128)S(1)} copy-done((f32[16,16,256]{2,1,0:T(8,128)S(1)}, f32[16,16,256]{2,1,0:T(8,128)}, u32[]{:S(2)}) %copy-start.8) | copy-done | bytes 262168
  20.7 0.9 %copy-done.9 = f32[16,16,256]{2,1,0:T(8,128)S(1)} copy-done((f32[16,16,256]{2,1,0:T(8,128)S(1)}, f32[16,16,256]{2,1,0:T(8,128)}, u32[]{:S(2)}) %copy-start.9) | copy-done | bytes 262168
  21.6 0.9 %copy-done.10 = f32[16,16,256]{2,1,0:T(8,128)S(1)} copy-done((f32[16,16,256]{2,1,0:T(8,128)S(1)}, f32[16,16,256]{2,1,0:T(8,128)}, u32[]{:S(2)}) %copy-start.10) | copy-done | bytes 262168
  23.3 0.7 copy-done.12
  24.7 1.7 %shard_map.158 = (f32[16,16,256]{2,1,0:T(8,128)}, f32[16,16,256]{2,1,0:T(8,128)}, bf16[8,32,128]{2,1,0:T(8,128)(2,1)}) custom-call(f32[16,16,256]{2,1,0:T(8,128)S(1)} %copy-done.6, f32[16,16,256]{2,1,0:T(8,128)S(1)} %copy-done.8, f32[16,16,256]{2,1,0:T(8,128)S(1)} %copy-done.9, f32[16,16,256]{2,1,0:T(8,128)S(1)} %copy-done.10, f32[16,256]{1,0:T(8,128)S(1)} %copy-done.11, ...), custom_call_target="tpu_custom_call" | custom-call | bytes 1572864 | tf_op jit(solution)/shard_map/pallas_call | solution.py:27
  26.5 6.0 %all-to-all-start = ((bf16[8,32,128]{2,1,0:T(8,128)(2,1)}), bf16[8,32,128]{2,1,0:T(8,128)(2,1)S(1)}, u32[]{:S(2)}, u32[]{:S(2)}) async-start(bf16[8,32,128]{2,1,0:T(8,128)(2,1)} %get-tuple-element.24), calls=%async_computation | async-start | bytes 131072 | tf_op jit(solution)/shard_map/all_to_all | solution.py:279
  32.5 4.7 %shard_map.159 = (bf16[2048,256]{1,0:T(8,128)(2,1)S(1)}, bf16[2048,256]{1,0:T(8,128)(2,1)S(1)}) custom-call(s32[16,128]{1,0:T(8,128)S(1)} %reshape.65.order, bf16[2048,256]{1,0:T(8,128)(2,1)S(1)} %bitcast.29, bf16[2048,256]{1,0:T(8,128)(2,1)S(1)} %bitcast.31), custom_call_target="tpu_custom_call" | custom-call | flops 4294967296 | bytes 4194304 | tf_op jit(solution)/shard_map/pallas_call | solution.py:27
  37.1 1.0 %copy-done.3 = bf16[2048,256]{1,0:T(8,128)(2,1)} copy-done((bf16[2048,256]{1,0:T(8,128)(2,1)}, bf16[2048,256]{1,0:T(8,128)(2,1)S(1)}, u32[]{:S(2)}) %copy-start.3) | copy-done | bytes 1048600
  38.1 1.2 %copy-done.4 = bf16[2048,256]{1,0:T(8,128)(2,1)S(1)} copy-done((bf16[2048,256]{1,0:T(8,128)(2,1)S(1)}, bf16[2048,256]{1,0:T(8,128)(2,1)}, u32[]{:S(2)}) %copy-start.4) | copy-done | bytes 1048600
  40.0 1.0 %copy-done.2 = bf16[2048,256]{1,0:T(8,128)(2,1)} copy-done((bf16[2048,256]{1,0:T(8,128)(2,1)}, bf16[2048,256]{1,0:T(8,128)(2,1)S(1)}, u32[]{:S(2)}) %copy-start.2) | copy-done | bytes 1048600
  40.9 5.1 %all-to-all-start.1 = ((bf16[8,256,256]{2,1,0:T(8,128)(2,1)}), bf16[8,256,256]{2,1,0:T(8,128)(2,1)S(1)}, u32[]{:S(2)}, u32[]{:S(2)}) async-start(bf16[8,256,256]{2,1,0:T(8,128)(2,1)} %bitcast.35), calls=%async_computation.1 | async-start | bytes 2097152 | tf_op jit(solution)/shard_map/all_to_all | solution.py:289
  46.1 25.7 %all-to-all-done.1 = bf16[8,256,256]{2,1,0:T(8,128)(2,1)S(1)} async-done(((bf16[8,256,256]{2,1,0:T(8,128)(2,1)}), bf16[8,256,256]{2,1,0:T(8,128)(2,1)S(1)}, u32[]{:S(2)}, u32[]{:S(2)}) %all-to-all-start.1) | async-done | bytes 1048608 | tf_op jit(solution)/shard_map/all_to_all | solution.py:289
  72.5 0.9 %collective-permute-start.4 = (bf16[512,256]{1,0:T(8,128)(2,1)S(1)}, bf16[512,256]{1,0:T(8,128)(2,1)}, u32[]{:S(2)}, u32[]{:S(2)}) collective-permute-start(bf16[512,256]{1,0:T(8,128)(2,1)S(1)} %shard_map.163), channel_id=1, source_target_pairs={{0,1},{1,0},{2,3},{3,2},{4,5},{5,4},{6,7},{7,6},{8,9},{9,8},{10,11... | collective-permute-start | bytes 786440 | tf_op jit(solution)/shard_map/ppermute | solution.py:314
  73.4 1.7 %shard_map.161 = bf16[2048,256]{1,0:T(8,128)(2,1)} custom-call(f32[16,128]{1,0:T(8,128)S(1)} %get-tuple-element.28.runoff, bf16[2048,256]{1,0:T(8,128)(2,1)S(1)} %bitcast.30, bf16[2048,256]{1,0:T(8,128)(2,1)S(1)} %bitcast.32), custom_call_target="tpu_custom_call" | custom-call | bytes 3145728 | tf_op jit(solution)/shard_map/pallas_call | solution.py:27
  75.9 1.8 %add_bitcast_fusion = f32[1,512,256]{2,1,0:T(8,128)} fusion(f32[512,256]{1,0:T(8,128)S(1)} %shard_map.162, bf16[512,256]{1,0:T(8,128)(2,1)} %collective-permute-done.4), kind=kLoop, calls=%fused_computation | loop fusion | flops 262144 | bytes 1310720 | tf_op jit(solution)/shard_map/broadcast_in_dim | solution.py:324
  (49 shorter events, 5.9 us)
Async XLA Ops:
  0.6 31.8 %copy-start = (bf16[1,2048,256]{2,1,0:T(8,128)(2,1)S(1)}, bf16[1,2048,256]{2,1,0:T(8,128)(2,1)}, u32[]{:S(2)}) copy-start(bf16[1,2048,256]{2,1,0:T(8,128)(2,1)} %param.20) | copy-start | bytes 3145732
  0.6 1.0 %copy-start.5 = (f32[16,16,256]{2,1,0:T(8,128)S(1)}, f32[16,16,256]{2,1,0:T(8,128)}, u32[]{:S(2)}) copy-start(f32[16,16,256]{2,1,0:T(8,128)} %moist.3) | copy-start | bytes 786436
  1.7 0.9 %copy-start.7 = (f32[16,16,256]{2,1,0:T(8,128)S(1)}, f32[16,16,256]{2,1,0:T(8,128)}, u32[]{:S(2)}) copy-start(f32[16,16,256]{2,1,0:T(8,128)} %heat.3) | copy-start | bytes 786436
  2.6 29.8 %copy-start.1 = (bf16[1,2048,256]{2,1,0:T(8,128)(2,1)S(1)}, bf16[1,2048,256]{2,1,0:T(8,128)(2,1)}, u32[]{:S(2)}) copy-start(bf16[1,2048,256]{2,1,0:T(8,128)(2,1)} %param.21) | copy-start | bytes 3145732
  2.8 15.9 %collective-permute-start = (bf16[32,256]{1,0:T(8,128)(2,1)S(1)}, bf16[32,256]{1,0:T(8,128)(2,1)S(1)}, u32[]{:S(2)}, u32[]{:S(2)}) collective-permute-start(bf16[32,256]{1,0:T(8,128)(2,1)S(1)} %get-tuple-element.17), channel_id=1, source_target_pairs={{0,1},{1,2},{2,3},{3,4},{4,5},{5,6},{6,7},{8,9},{9,10},{10,11},{11... | collective-permute-start | bytes 49160 | tf_op jit(solution)/shard_map/ppermute | solution.py:232
  6.7 12.0 %collective-permute-start.1 = (bf16[32,256]{1,0:T(8,128)(2,1)S(1)}, bf16[32,256]{1,0:T(8,128)(2,1)S(1)}, u32[]{:S(2)}, u32[]{:S(2)}) collective-permute-start(bf16[32,256]{1,0:T(8,128)(2,1)S(1)} %get-tuple-element.18), channel_id=1, source_target_pairs={{1,0},{2,1},{3,2},{4,3},{5,4},{6,5},{7,6},{9,8},{10,9},{11,10},{12... | collective-permute-start | bytes 49160 | tf_op jit(solution)/shard_map/ppermute | solution.py:233
  8.6 10.1 %collective-permute-start.2 = (bf16[16,128]{1,0:T(8,128)(2,1)S(1)}, bf16[16,128]{1,0:T(8,128)(2,1)S(1)}, u32[]{:S(2)}, u32[]{:S(2)}) collective-permute-start(bf16[16,128]{1,0:T(8,128)(2,1)S(1)} %get-tuple-element.19), channel_id=1, source_target_pairs={{0,8},{8,16},{16,24},{1,9},{9,17},{17,25},{2,10},{10,18},{18,26},{... | collective-permute-start | bytes 12296 | tf_op jit(solution)/shard_map/ppermute | solution.py:234
  11.8 7.0 %collective-permute-start.3 = (bf16[16,128]{1,0:T(8,128)(2,1)S(1)}, bf16[16,128]{1,0:T(8,128)(2,1)S(1)}, u32[]{:S(2)}, u32[]{:S(2)}) collective-permute-start(bf16[16,128]{1,0:T(8,128)(2,1)S(1)} %get-tuple-element.20), channel_id=1, source_target_pairs={{8,0},{16,8},{24,16},{9,1},{17,9},{25,17},{10,2},{18,10},{26,18},{... | collective-permute-start | bytes 12296 | tf_op jit(solution)/shard_map/ppermute | solution.py:235
  15.6 0.7 copy-start.14
  16.3 0.7 copy-start.15
  17.0 0.7 copy-start.16
  18.8 1.0 %copy-start.6 = (f32[16,16,256]{2,1,0:T(8,128)S(1)}, f32[16,16,256]{2,1,0:T(8,128)}, u32[]{:S(2)}) copy-start(f32[16,16,256]{2,1,0:T(8,128)} %moist.3) | copy-start | bytes 786436
  19.7 0.9 %copy-start.8 = (f32[16,16,256]{2,1,0:T(8,128)S(1)}, f32[16,16,256]{2,1,0:T(8,128)}, u32[]{:S(2)}) copy-start(f32[16,16,256]{2,1,0:T(8,128)} %heat.3) | copy-start | bytes 786436
  20.7 0.9 %copy-start.9 = (f32[16,16,256]{2,1,0:T(8,128)S(1)}, f32[16,16,256]{2,1,0:T(8,128)}, u32[]{:S(2)}) copy-start(f32[16,16,256]{2,1,0:T(8,128)} %moist_k.1) | copy-start | bytes 786436
  21.6 0.9 %copy-start.10 = (f32[16,16,256]{2,1,0:T(8,128)S(1)}, f32[16,16,256]{2,1,0:T(8,128)}, u32[]{:S(2)}) copy-start(f32[16,16,256]{2,1,0:T(8,128)} %heat_k.1) | copy-start | bytes 786436
  22.6 0.7 copy-start.11
  23.3 0.7 copy-start.12
  24.0 0.7 copy-start.13
  26.5 11.7 %all-to-all-start = ((bf16[8,32,128]{2,1,0:T(8,128)(2,1)}), bf16[8,32,128]{2,1,0:T(8,128)(2,1)S(1)}, u32[]{:S(2)}, u32[]{:S(2)}) async-start(bf16[8,32,128]{2,1,0:T(8,128)(2,1)} %get-tuple-element.24), calls=%async_computation | async-start | bytes 131072 | tf_op jit(solution)/shard_map/all_to_all | solution.py:279
  37.1 1.0 %copy-start.3 = (bf16[2048,256]{1,0:T(8,128)(2,1)}, bf16[2048,256]{1,0:T(8,128)(2,1)S(1)}, u32[]{:S(2)}) copy-start(bf16[2048,256]{1,0:T(8,128)(2,1)S(1)} %get-tuple-element.27.hyd_packed) | copy-start | bytes 3145732
  38.1 1.2 %copy-start.4 = (bf16[2048,256]{1,0:T(8,128)(2,1)S(1)}, bf16[2048,256]{1,0:T(8,128)(2,1)}, u32[]{:S(2)}) copy-start(bf16[2048,256]{1,0:T(8,128)(2,1)} %copy-done.3) | copy-start | bytes 3145732
  40.0 1.0 %copy-start.2 = (bf16[2048,256]{1,0:T(8,128)(2,1)}, bf16[2048,256]{1,0:T(8,128)(2,1)S(1)}, u32[]{:S(2)}) copy-start(bf16[2048,256]{1,0:T(8,128)(2,1)S(1)} %get-tuple-element.29) | copy-start | bytes 3145732
  40.9 30.8 %all-to-all-start.1 = ((bf16[8,256,256]{2,1,0:T(8,128)(2,1)}), bf16[8,256,256]{2,1,0:T(8,128)(2,1)S(1)}, u32[]{:S(2)}, u32[]{:S(2)}) async-start(bf16[8,256,256]{2,1,0:T(8,128)(2,1)} %bitcast.35), calls=%async_computation.1 | async-start | bytes 2097152 | tf_op jit(solution)/shard_map/all_to_all | solution.py:289
  72.5 3.4 %collective-permute-start.4 = (bf16[512,256]{1,0:T(8,128)(2,1)S(1)}, bf16[512,256]{1,0:T(8,128)(2,1)}, u32[]{:S(2)}, u32[]{:S(2)}) collective-permute-start(bf16[512,256]{1,0:T(8,128)(2,1)S(1)} %shard_map.163), channel_id=1, source_target_pairs={{0,1},{1,0},{2,3},{3,2},{4,5},{5,4},{6,7},{7,6},{8,9},{9,8},{10,11... | collective-permute-start | bytes 786440 | tf_op jit(solution)/shard_map/ppermute | solution.py:314
